TPU v7x, 32 devices: a whole 2x2x4 slice. The times are simulated.
32 devices in a mesh: member: 16 (over z, y, x), mp: 2 (over core).
Axes of the slice: x: 2, y: 2, z: 4, core: 2. Of those that a mesh axis runs over, the one named last changes fastest.
Arguments:
- token_ids: int32 [64, 64], P('member'), may hold values from 0 to 76031
- fit_ranks: int32 [64], P('member'), may hold values from 0 to 63, as said below
- embed_table: bfloat16 [3584, 76032], P('member'), may hold values from -40 to 40
- norm_gain: float32 [3584], replicated, may hold values from 0.1 to 1.9
- qkv_weight: bfloat16 [3584, 2304], P('member', 'mp'), may hold values from -0.09375 to 0.09375
- qkv_bias: float32 [2304], P('mp'), may hold values from -3 to 3
- out_weight: bfloat16 [3584, 1792], P('member', 'mp'), may hold values from -0.125 to 0.125
- value_weight: float32 [3584], replicated, may hold values from -0.09375 to 0.09375
- qkv_left: bfloat16 [64, 3584], P('member'), may hold values from -5 to 5
- qkv_right: bfloat16 [64, 2304], P('member', 'mp'), may hold values from -5 to 5
- out_left: bfloat16 [64, 1792], P('member', 'mp'), may hold values from -5 to 5
- out_right: bfloat16 [64, 3584], P('member'), may hold values from -5 to 5
Outputs:
- values: float32 [64, 64], P(('member', 'mp'))
- qkv_grad: float32 [3584, 2304], P('member', 'mp')
- out_grad: float32 [3584, 1792], P('member', 'mp')
Inputs may be any that keep to these rules, and one draw needn't show every extreme that they name: `fit_ranks`: A member's rank is the number of members whose integer fitness score is strictly lower; equal scores share a rank.
All inputs are finite; a program needn't handle non-finite values.
Results may differ from a plain program's by a relative error of at most 0.0052.
Values may be sent and summed in bfloat16 or wider, within the bound.
A program may use at most 128 MiB of HBM per device.

v0:
```python
import math

import jax
import jax.numpy as jnp
from jax import lax
from jax.sharding import PartitionSpec as P

HD = 128
HQ = 14
HK = 2


SIGMA = 0.01
EPSILON = 1e-06
THETA = 1000000.0
MASKED = -1e30


def rope_tables(length, head_size):
    halfway = head_size // 2
    inverse = THETA ** (-(jnp.arange(halfway, dtype=jnp.float32) * 2.0 / head_size))
    places = jnp.arange(length, dtype=jnp.float32)
    angles = places[:, None] * inverse[None, :]
    angles = jnp.concatenate([angles, angles], axis=1)
    return (jnp.cos(angles), jnp.sin(angles))


def rotate(states, cosine, sine_table):
    halfway = states.shape[-1] // 2
    turned = jnp.concatenate([-states[..., halfway:], states[..., :halfway]], axis=-1)
    return states * cosine[None, :, None, :] + turned * sine_table[None, :, None, :]


def attend(query_heads, key_heads, value_heads, kv_count):
    members, length, head_count, head_size = query_heads.shape
    group_size = head_count // kv_count
    grouped = query_heads.reshape(members, length, kv_count, group_size, head_size)
    scores = jnp.einsum(
        "mskgd,mtkd->mkgst", grouped, key_heads, preferred_element_type=jnp.float32
    ) / math.sqrt(head_size)
    causal = jnp.arange(length)[None, :] <= jnp.arange(length)[:, None]
    scores = jnp.where(causal, scores, MASKED)
    top = jnp.max(scores, axis=-1, keepdims=True)
    weights = jnp.exp(scores - top)
    weights = (weights / jnp.sum(weights, axis=-1, keepdims=True)).astype(jnp.bfloat16)
    context = jnp.einsum(
        "mkgst,mtkd->mskgd", weights, value_heads, preferred_element_type=jnp.float32
    )
    return context.astype(jnp.bfloat16).reshape(members, length, head_count * head_size)


def on_device(
    token_ids,
    fit_ranks,
    embed_table,
    norm_gain,
    qkv_weight,
    qkv_bias,
    out_weight,
    value_weight,
    qkv_left,
    qkv_right,
    out_left,
    out_right,
):
    members, length = token_ids.shape
    row_count = members * length
    mp_size = lax.axis_size("mp")
    heads_here = HQ // mp_size
    kv_here = HK // mp_size
    population = members * lax.axis_size("member")
    contract_rows = (((0,), (0,)), ((), ()))
    contract_cols = (((1,), (1,)), ((), ()))
    all_ids = lax.all_gather(token_ids, "member", axis=0, tiled=True)
    picked = jnp.take(embed_table, all_ids.reshape(-1), axis=1)
    embedded = lax.all_to_all(picked, "member", split_axis=1, concat_axis=0, tiled=True)
    features = embedded.astype(jnp.float32)
    inverse_rms = lax.rsqrt(jnp.mean(features * features, axis=0, keepdims=True) + EPSILON)
    normed = (features * inverse_rms * norm_gain[:, None]).astype(jnp.bfloat16)
    base_proj = lax.dot_general(
        normed,
        lax.all_gather(qkv_weight, "member", axis=0, tiled=True),
        contract_rows,
        preferred_element_type=jnp.float32,
    )
    normed_members = normed.reshape(normed.shape[0], members, length)
    coef_in = jnp.einsum("dms,md->ms", normed_members, qkv_left, preferred_element_type=jnp.float32)
    projected = (
        base_proj.reshape(members, length, -1)
        + SIGMA * coef_in[:, :, None] * qkv_right.astype(jnp.float32)[:, None, :]
        + qkv_bias[None, None, :]
    )
    query_width = heads_here * HD
    kv_width = kv_here * HD
    cosine, sine_table = rope_tables(length, HD)
    query_heads = rotate(
        projected[:, :, :query_width].reshape(members, length, heads_here, HD), cosine, sine_table
    ).astype(jnp.bfloat16)
    key_heads = rotate(
        projected[:, :, query_width : query_width + kv_width].reshape(members, length, kv_here, HD),
        cosine,
        sine_table,
    ).astype(jnp.bfloat16)
    value_heads = (
        projected[:, :, query_width + kv_width :]
        .reshape(members, length, kv_here, HD)
        .astype(jnp.bfloat16)
    )
    context = attend(query_heads, key_heads, value_heads, kv_here)
    coef_out = jnp.einsum("msq,mq->ms", context, out_left, preferred_element_type=jnp.float32)
    flat_context = context.reshape(row_count, query_width)
    share_rows = row_count // mp_size
    partial_out = lax.dot_general(
        flat_context,
        lax.all_gather(out_weight, "member", axis=0, tiled=True),
        contract_cols,
        preferred_element_type=jnp.float32,
    )
    head_term = (
        partial_out.reshape(members, length, -1)
        + SIGMA * coef_out[:, :, None] * out_right.astype(jnp.float32)[:, None, :]
    )
    summed = lax.psum_scatter(
        head_term.reshape(row_count, -1), "mp", scatter_dimension=0, tiled=True
    )
    mp_index = lax.axis_index("mp")
    own_embed = lax.dynamic_slice_in_dim(embedded, mp_index * share_rows, share_rows, 1)
    residual = own_embed.T.astype(jnp.float32) + summed
    inverse_out = lax.rsqrt(jnp.mean(residual * residual, axis=1, keepdims=True) + EPSILON)
    value_rows = jnp.sum(residual * inverse_out * value_weight[None, :], axis=1).reshape(
        members // mp_size, length
    )
    rank_values = fit_ranks.astype(jnp.float32)
    first_sum, second_sum = lax.psum(
        (jnp.sum(rank_values), jnp.sum(rank_values * rank_values)), "member"
    )
    center = first_sum / population
    spread = second_sum / population - center * center
    fit_local = (rank_values - center) * lax.rsqrt(spread + EPSILON)
    fitness = lax.all_gather(fit_local, "member", axis=0, tiled=True)
    left_rows, right_rows = (
        lax.all_to_all(qkv_left, "member", split_axis=1, concat_axis=0, tiled=True),
        lax.all_to_all(out_right, "member", split_axis=1, concat_axis=0, tiled=True),
    )
    right_cols, left_cols = (
        lax.all_gather(qkv_right, "member", axis=0, tiled=True),
        lax.all_gather(out_left, "member", axis=0, tiled=True),
    )
    weighted_in = left_rows.astype(jnp.float32) * fitness[:, None]
    qkv_grad = lax.dot_general(
        weighted_in,
        right_cols.astype(jnp.float32),
        contract_rows,
        precision=lax.Precision.HIGHEST,
        preferred_element_type=jnp.float32,
    ) / (population * SIGMA)
    weighted_out = right_rows.astype(jnp.float32) * fitness[:, None]
    out_grad = lax.dot_general(
        weighted_out,
        left_cols.astype(jnp.float32),
        contract_rows,
        precision=lax.Precision.HIGHEST,
        preferred_element_type=jnp.float32,
    ) / (population * SIGMA)
    return (value_rows, qkv_grad, out_grad)


def solution(mesh):
    placed = (
        P("member", None),
        P("member"),
        P("member", None),
        P(),
        P("member", "mp"),
        P("mp"),
        P("member", "mp"),
        P(),
        P("member", None),
        P("member", "mp"),
        P("member", "mp"),
        P("member", None),
    )
    return jax.shard_map(
        on_device,
        mesh=mesh,
        in_specs=placed,
        out_specs=(P(("member", "mp"), None), P("member", "mp"), P("member", "mp")),
        check_vma=False,
    )
```

profile of v0, /device:TPU:0, one launch (start us, length us, event | category | flops | bytes accessed | tf_op | source)
XLA Modules:
  0.0 446.2 jit_solution(1839496183374414242)
XLA Ops:
  8.6 43.4 %all-gather = s32[16,4,64]{2,1,0:T(4,128)S(1)} all-gather(s32[1,4,64]{2,1,0:T(4,128)} %bitcast.98), channel_id=1, replica_groups=mesh['member'=16,'mp'=2] {'member'}, dimensions={0}, use_global_device_ids=true | all-gather | bytes 17408 | tf_op jit(solution)/shard_map/all_gather | solution.py:74
  52.3 44.6 %copy.41 = bf16[224,76032]{0,1:T(8,128)(2,1)} copy(bf16[224,76032]{1,0:T(8,128)(2,1)} %param.14) | data formatting | bytes 68124672 | tf_op args[2]
  96.9 44.1 %gather_fusion = bf16[4096,224]{1,0:T(8,128)(2,1)S(1)} fusion(bf16[224,76032]{0,1:T(8,128)(2,1)} %copy.41, s32[4096]{0:T(1024)S(1)} %broadcast_clamp_fusion), kind=kCustom, calls=%fused_computation | custom fusion | bytes 3686400 | tf_op jit(solution)/shard_map/jit(_take)/gather | solution.py:75
  141.1 2.4 copy.42
  143.4 2.9 broadcast_select_fusion
  146.4 3.8 all-to-all-start
  150.6 51.5 %all-to-all-done = bf16[224,16,256]{2,0,1:T(8,128)(2,1)S(1)} async-done(((bf16[224,16,256]{2,0,1:T(8,128)(2,1)}), bf16[224,16,256]{2,0,1:T(8,128)(2,1)S(1)}, u32[]{:S(2)}, u32[]{:S(2)}) %all-to-all-start) | async-done | bytes 1835040 | tf_op jit(solution)/shard_map/all_to_all | solution.py:76
  202.7 2.2 bitcast_convert_fusion
  204.9 5.4 %copy.44 = f32[16,224,256]{1,0,2:T(8,128)} copy(f32[16,224,256]{2,1,0:T(8,128)} %bitcast_convert_fusion) | data formatting | bytes 7340032 | tf_op jit(solution)/shard_map/convert_element_type | solution.py:77
  210.3 5.6 %reshape.204 = f32[3584,4,64]{0,2,1:T(8,128)} reshape(f32[16,224,256]{1,0,2:T(8,128)} %copy.44) | data formatting | bytes 7340032 | tf_op jit(solution)/shard_map/convert_element_type | solution.py:77
  215.8 2.5 fusion.13
  218.3 3.9 copy.43
  222.2 2.7 fusion.14
  224.9 6.5 %fusion.10 = f32[4,64,1152]{2,1,0:T(8,128)S(1)} fusion(bf16[4,64,3584]{2,1,0:T(8,128)(2,1)} %bitcast.91, bf16[3584,1152]{1,0:T(8,128)(2,1)} %all-gather.6.cloned.1.call-done, f32[1152]{0:T(1024)S(1)} %copy-done.9, f32[4,1152]{1,0:T(4,128)S(1)} %convert_element_type.84, f32[4,64]{1,0:T(4,128)S(1)} %broadcast_multiply_fusion.1), kind=kOutput, calls=%fused_computation.10 | convolution fusion | flops 2114813952 | bytes 11296256 | tf_op jit(solution)/shard_map/dot_general | solution.py:80
  240.6 6.0 %all-gather.8.cloned.1.call-done = bf16[3584,896]{1,0:T(8,128)(2,1)} async-done(((bf16[224,896]{1,0:T(8,128)(2,1)}), bf16[3584,896]{1,0:T(8,128)(2,1)}) %all-gather.8.cloned.1.call-update) | async-done | bytes 6422544 | tf_op jit(solution)/shard_map/all_gather | solution.py:115
  246.6 6.7 %fusion.4 = f32[4,64,3584]{2,1,0:T(8,128)} fusion(bf16[4,64,896]{2,1,0:T(8,128)(2,1)S(1)} %dot_general.36, bf16[3584,896]{1,0:T(8,128)(2,1)} %all-gather.8.cloned.1.call-done, f32[4,3584]{1,0:T(4,128)S(1)} %convert_element_type.91, f32[4,64]{1,0:T(4,128)S(1)} %broadcast_multiply_fusion), kind=kOutput, calls=%fused_computation.5 | convolution fusion | flops 1646002176 | bytes 10609664 | tf_op jit(solution)/shard_map/dot_general | solution.py:113
  253.3 5.1 %copy.48 = f32[256,3584]{0,1:T(8,128)} copy(f32[256,3584]{1,0:T(8,128)} %bitcast.90) | data formatting | bytes 7340032 | tf_op jit(solution)/shard_map/reshape | solution.py:124
  259.2 3.9 all-to-all-start.1
  263.7 42.7 %all-reduce.1 = (f32[]{:T(128)}, f32[]{:T(128)}) all-reduce(f32[]{:T(128)} %get-tuple-element.4, f32[]{:T(128)} %get-tuple-element.3), channel_id=1, replica_groups=mesh['member'=16,'mp'=2] {'member'}, use_global_device_ids=true, to_apply=%region_9.10 | all-reduce | flops 2 | bytes 16 | tf_op jit(solution)/shard_map/psum | solution.py:134
  309.2 36.2 %all-gather.1 = bf16[16,4,1152]{2,1,0:T(4,128)(2,1)S(1)} all-gather(bf16[1,4,1152]{2,1,0:T(4,128)(2,1)S(1)} %bitcast.94), channel_id=1, replica_groups=mesh['member'=16,'mp'=2] {'member'}, dimensions={0}, use_global_device_ids=true | all-gather | bytes 156672 | tf_op jit(solution)/shard_map/all_gather | solution.py:146
  346.8 38.2 %all-gather.2 = bf16[16,4,896]{2,1,0:T(4,128)(2,1)S(1)} all-gather(bf16[1,4,896]{2,1,0:T(4,128)(2,1)S(1)} %bitcast.97), channel_id=1, replica_groups=mesh['member'=16,'mp'=2] {'member'}, dimensions={0}, use_global_device_ids=true | all-gather | bytes 121856 | tf_op jit(solution)/shard_map/all_gather | solution.py:147
  385.7 36.5 %all-reduce = f32[64]{0:T(128)S(1)} all-reduce(f32[64]{0:T(128)S(1)} %multiply_dynamic-update-slice_fusion), channel_id=1, replica_groups=mesh['member'=16,'mp'=2] {'member'}, use_global_device_ids=true, to_apply=%add | all-reduce | flops 64 | bytes 512
  422.2 3.5 all-to-all-start.2
  425.8 7.3 %all-to-all-done.2 = bf16[4,16,224]{2,0,1:T(4,128)(2,1)S(1)} async-done(((bf16[4,16,224]{2,0,1:T(4,128)(2,1)}), bf16[4,16,224]{2,0,1:T(4,128)(2,1)S(1)}, u32[]{:S(2)}, u32[]{:S(2)}) %all-to-all-start.2) | async-done | bytes 28704 | tf_op jit(solution)/shard_map/all_to_all | solution.py:143
  (79 shorter events, 21.1 us)
Async XLA Ops:
  7.2 217.7 %all-gather.6.cloned.1.call-start = ((), (), s32[]{:S(2)}) async-start(), calls=%async_computation.4 | async-start | bytes 8773632 | tf_op jit(solution)/shard_map/all_gather | solution.py:82
  7.9 238.7 %all-gather.8.cloned.1.call-start = ((), (), s32[]{:S(2)}) async-start(), calls=%async_computation.5 | async-start | bytes 6823936 | tf_op jit(solution)/shard_map/all_gather | solution.py:115
  146.4 3.9 copy-start.5
  146.4 3.9 copy-start.3
  146.4 55.7 %all-to-all-start = ((bf16[224,16,256]{2,0,1:T(8,128)(2,1)}), bf16[224,16,256]{2,0,1:T(8,128)(2,1)S(1)}, u32[]{:S(2)}, u32[]{:S(2)}) async-start(bf16[224,16,256]{2,0,1:T(8,128)(2,1)} %broadcast_select_fusion), calls=%async_computation | async-start | bytes 3670016 | tf_op jit(solution)/shard_map/all_to_all | solution.py:76
  150.2 286.1 %reduce-scatter.2.cloned.1.call-start = ((), (), s32[]{:S(2)}) async-start(), calls=%async_computation.6 | async-start | bytes 5505024 | tf_op jit(solution)/shard_map/reduce_scatter | solution.py:123
  210.3 5.6 %copy-start.4 = (f32[3584]{0:T(1024)S(1)}, f32[3584]{0:T(1024)}, u32[]{:S(2)}) copy-start(f32[3584]{0:T(1024)} %param.15) | copy-start | bytes 43012
  218.3 3.9 copy-start.2
  222.2 2.7 copy-start.9
  231.4 1.0 copy-start.1
  239.5 0.9 copy-start.7
  258.4 4.7 %copy-start.8 = (s32[4]{0:T(128)S(1)}, s32[4]{0:T(128)}, u32[]{:S(2)}) copy-start(s32[4]{0:T(128)} %param.13) | copy-start | bytes 52
  258.4 87.0 %copy-start.10 = (u32[32]{0:T(128)S(1)}, u32[32]{0:T(128)}, u32[]{:S(2)}) copy-start(u32[32]{0:T(128)} %constant.70) | copy-start | bytes 388
  259.2 163.0 %all-to-all-start.1 = ((bf16[4,16,224]{2,0,1:T(4,128)(2,1)}), bf16[4,16,224]{2,0,1:T(4,128)(2,1)S(1)}, u32[]{:S(2)}, u32[]{:S(2)}) async-start(bf16[4,16,224]{2,0,1:T(4,128)(2,1)} %copy.49), calls=%async_computation.2 | async-start | bytes 65536 | tf_op jit(solution)/shard_map/all_to_all | solution.py:142
  422.2 10.9 %all-to-all-start.2 = ((bf16[4,16,224]{2,0,1:T(4,128)(2,1)}), bf16[4,16,224]{2,0,1:T(4,128)(2,1)S(1)}, u32[]{:S(2)}, u32[]{:S(2)}) async-start(bf16[4,16,224]{2,0,1:T(4,128)(2,1)} %copy.50), calls=%async_computation.3 | async-start | bytes 65536 | tf_op jit(solution)/shard_map/all_to_all | solution.py:143
  434.6 3.8 copy-start.6
  436.3 2.1 copy-start
Sparse Core Ops, SparseCore 0:
  10.8 114.6 all-gather.5
  128.2 118.3 all-gather.7
  258.6 9.8 reduce-scatter.1
where the time goes:
time: 449 us; the launch traced here: 446 us
  blocking collectives  197 us (44%)
  local copies, waits for them, and re-layouts  119 us (27%)
  waiting for transfers between devices  66.2 us (15%)
  matrix products  22 us (5%)
  between operations  17.3 us (4%)
  other arithmetic  12.9 us (3%)
  starting transfers between devices  11.4 us (3%)
    all_to_all x1, waiting for transfers between devices, on_device(): lax.all_to_all(picked, 'member', split_axis=1, concat_axis=0, tiled=True)  51.5 us
    gather x2, local copies, waits for them, and re-layouts, on_device(): picked = jnp.take(embed_table, all_ids.reshape(-1), axis=1)  46.5 us
    unnamed x27, local copies, waits for them, and re-layouts  46.3 us
    all_gather x1, blocking collectives, on_device(): all_ids = lax.all_gather(token_ids, 'member', axis=0, tiled=True)  43.4 us
    psum x1, blocking collectives, on_device(): lax.psum((jnp.sum(rank_values), jnp.sum(rank_values * rank_values)), 'mem...  42.7 us
    all_gather x1, blocking collectives, on_device(): lax.all_gather(out_left, 'member', axis=0, tiled=True)  38.2 us
    unnamed x1, blocking collectives  36.5 us
    all_gather x1, blocking collectives, on_device(): lax.all_gather(qkv_right, 'member', axis=0, tiled=True)  36.2 us
  transfers between devices with their start and end apart: 6, of which 3 were waited for; matrix products, arithmetic and copies ran while one was open for 31% of the time, Pallas kernels for 0%

commit v1 on v0

--- a/solution.py
+++ b/solution.py
@@ -1,8 +1,11 @@
+import functools
 import math
 
 import jax
 import jax.numpy as jnp
 from jax import lax
+from jax.experimental import pallas as pl
+from jax.experimental.pallas import tpu as pltpu
 from jax.sharding import PartitionSpec as P
 
 HD = 128
@@ -165,6 +168,441 @@
     return (value_rows, qkv_grad, out_grad)
 
 
+MESH = pl.DeviceIdType.MESH
+VOCAB_BLOCK = 2304
+GROUP = 256
+MIB = 1024 * 1024
+
+
+def share_kernel(n, ids_ref, pack_ref, all_ids_ref, all_pack_ref, send_sem, recv_sem, own_sem):
+    me = lax.axis_index("member")
+    core = lax.axis_index("mp")
+    barrier = pltpu.get_barrier_semaphore()
+
+    def greet(k, carry):
+        other = lax.rem(me + k, n)
+        pl.semaphore_signal(barrier, inc=1, device_id=(other, core), device_id_type=MESH)
+        return carry
+
+    lax.fori_loop(1, n, greet, 0)
+    pl.semaphore_wait(barrier, n - 1)
+
+    def copies(k):
+        other = lax.rem(me + k, n)
+        return (
+            pltpu.make_async_remote_copy(
+                src_ref=ids_ref,
+                dst_ref=all_ids_ref.at[me],
+                send_sem=send_sem.at[0, k],
+                recv_sem=recv_sem.at[0, k],
+                device_id=(other, core),
+                device_id_type=MESH,
+            ),
+            pltpu.make_async_remote_copy(
+                src_ref=pack_ref.at[other],
+                dst_ref=all_pack_ref.at[me],
+                send_sem=send_sem.at[1, k],
+                recv_sem=recv_sem.at[1, k],
+                device_id=(other, core),
+                device_id_type=MESH,
+            ),
+        )
+
+    def launch(k, carry):
+        for copy in copies(k):
+            copy.start()
+        return carry
+
+    lax.fori_loop(1, n, launch, 0)
+    own_ids = pltpu.make_async_copy(ids_ref, all_ids_ref.at[me], own_sem.at[0])
+    own_pack = pltpu.make_async_copy(pack_ref.at[me], all_pack_ref.at[me], own_sem.at[1])
+    own_ids.start()
+    own_pack.start()
+    own_ids.wait()
+    own_pack.wait()
+
+    def finish(k, carry):
+        for copy in copies(k):
+            copy.wait()
+        return carry
+
+    lax.fori_loop(1, n, finish, 0)
+
+
+def share(ids, pack, n):
+    return pl.pallas_call(
+        functools.partial(share_kernel, n),
+        out_shape=(
+            jax.ShapeDtypeStruct((n,) + ids.shape, ids.dtype),
+            jax.ShapeDtypeStruct(pack.shape, pack.dtype),
+        ),
+        in_specs=[pl.BlockSpec(memory_space=pltpu.VMEM)] * 2,
+        out_specs=[pl.BlockSpec(memory_space=pltpu.VMEM)] * 2,
+        scratch_shapes=[
+            pltpu.SemaphoreType.DMA((2, n)),
+            pltpu.SemaphoreType.DMA((2, n)),
+            pltpu.SemaphoreType.DMA((2,)),
+        ],
+        compiler_params=pltpu.CompilerParams(collective_id=0, has_side_effects=True),
+        name="share_small",
+    )(ids, pack)
+
+
+def pick_kernel(count_ref, sorted_ref, rank_ref, table_ref, out_ref, total):
+    step = pl.program_id(0)
+    last = pl.num_programs(0) - 1
+    picks = total.shape[1]
+    width = table_ref.shape[1]
+
+    @pl.when(step == 0)
+    def _():
+        total[...] = jnp.zeros_like(total)
+
+    first = count_ref[step] // GROUP
+    final = (count_ref[step + 1] + GROUP - 1) // GROUP
+
+    def group_step(g, carry):
+        columns = pl.ds(pl.multiple_of(g * GROUP, GROUP), GROUP)
+        local = sorted_ref[:, columns] - step * width
+        entries = lax.broadcasted_iota(jnp.int32, (width, GROUP), 0)
+        chosen = jnp.where(entries == local, 1.0, 0.0).astype(jnp.bfloat16)
+        total[:, columns] += jnp.dot(
+            table_ref[...], chosen, preferred_element_type=jnp.float32
+        )
+        return carry
+
+    lax.fori_loop(first, final, group_step, 0)
+
+    @pl.when(step == last)
+    def _():
+        found = total[...].astype(jnp.bfloat16)
+        block = out_ref.shape[2]
+        for g in range(picks // GROUP):
+            ranks = rank_ref[:, g * GROUP : (g + 1) * GROUP]
+            places = lax.broadcasted_iota(jnp.int32, (picks, GROUP), 0)
+            moved = jnp.where(places == ranks, 1.0, 0.0).astype(jnp.bfloat16)
+            back = jnp.dot(found, moved, preferred_element_type=jnp.float32).astype(jnp.bfloat16)
+            for part in range(GROUP // block):
+                out_ref[g * (GROUP // block) + part] = back[:, part * block : (part + 1) * block]
+
+
+def pick_columns(table, ids, block):
+    features, vocabulary = table.shape
+    picks = ids.shape[0]
+    steps = vocabulary // VOCAB_BLOCK
+    keys = ids * picks + jnp.arange(picks, dtype=jnp.int32)
+    ranks = jnp.sum((keys[None, :] < keys[:, None]).astype(jnp.int32), axis=1)
+    places = jnp.arange(picks, dtype=jnp.int32)
+    ordered = jnp.sum(jnp.where(ranks[None, :] == places[:, None], ids[None, :], 0), axis=1)
+    edges = jnp.arange(steps + 1, dtype=jnp.int32) * VOCAB_BLOCK
+    counts = jnp.sum((ids[None, :] < edges[:, None]).astype(jnp.int32), axis=1)
+    return pl.pallas_call(
+        pick_kernel,
+        out_shape=jax.ShapeDtypeStruct((picks // block, features, block), jnp.bfloat16),
+        grid_spec=pltpu.PrefetchScalarGridSpec(
+            num_scalar_prefetch=1,
+            grid=(steps,),
+            in_specs=[
+                pl.BlockSpec((1, picks), lambda i, c: (0, 0)),
+                pl.BlockSpec((1, picks), lambda i, c: (0, 0)),
+                pl.BlockSpec((features, VOCAB_BLOCK), lambda i, c: (0, i)),
+            ],
+            out_specs=pl.BlockSpec((picks // block, features, block), lambda i, c: (0, 0, 0)),
+            scratch_shapes=[pltpu.VMEM((features, picks), jnp.float32)],
+        ),
+        compiler_params=pltpu.CompilerParams(
+            vmem_limit_bytes=40 * MIB, dimension_semantics=("arbitrary",)
+        ),
+        cost_estimate=pl.CostEstimate(
+            flops=2 * features * vocabulary * GROUP,
+            bytes_accessed=features * vocabulary * 2,
+            transcendentals=0,
+        ),
+        name="pick_columns",
+    )(counts, ordered[None, :], ranks[None, :], table)
+
+
+def deliver_kernel(n, blocks_ref, out_ref, send_sem, recv_sem, pass_send, pass_recv, own_sem):
+    me = lax.axis_index("member")
+    core = lax.axis_index("mp")
+    features, block = blocks_ref.shape[1:]
+    barrier = pltpu.get_barrier_semaphore()
+    partner = (me, 1 - core)
+
+    def greet(k, carry):
+        other = lax.rem(me + k, n)
+        pl.semaphore_signal(barrier, inc=1, device_id=(other, core), device_id_type=MESH)
+        return carry
+
+    lax.fori_loop(1, n, greet, 0)
+    pl.semaphore_signal(barrier, inc=1, device_id=partner, device_id_type=MESH)
+    pl.semaphore_wait(barrier, n)
+    columns = pl.ds(pl.multiple_of(core * block, block), block)
+
+    def place(source):
+        return out_ref.at[pl.ds(pl.multiple_of(source * features, 16), features), columns]
+
+    def across(k):
+        other = lax.rem(me + k, n)
+        return pltpu.make_async_remote_copy(
+            src_ref=blocks_ref.at[other],
+            dst_ref=place(me),
+            send_sem=send_sem.at[k],
+            recv_sem=recv_sem.at[k],
+            device_id=(other, core),
+            device_id_type=MESH,
+        )
+
+    def over(k, source_ref, source):
+        return pltpu.make_async_remote_copy(
+            src_ref=source_ref,
+            dst_ref=place(source),
+            send_sem=pass_send.at[k],
+            recv_sem=pass_recv.at[k],
+            device_id=partner,
+            device_id_type=MESH,
+        )
+
+    def launch(k, carry):
+        across(k).start()
+        return carry
+
+    lax.fori_loop(1, n, launch, 0)
+    over(0, blocks_ref.at[me], me).start()
+    own = pltpu.make_async_copy(blocks_ref.at[me], place(me), own_sem)
+    own.start()
+
+    def forward(k, carry):
+        across(k).wait_recv()
+        source = lax.rem(me + n - k, n)
+        over(k, place(source), source).start()
+        return carry
+
+    lax.fori_loop(1, n, forward, 0)
+    own.wait()
+    over(0, blocks_ref.at[me], me).wait()
+
+    def finish(k, carry):
+        across(k).wait_send()
+        source = lax.rem(me + n - k, n)
+        over(k, place(source), source).wait()
+        return carry
+
+    lax.fori_loop(1, n, finish, 0)
+
+
+def deliver(blocks, n):
+    _, features, block = blocks.shape
+    return pl.pallas_call(
+        functools.partial(deliver_kernel, n),
+        out_shape=jax.ShapeDtypeStruct((n * features, 2 * block), blocks.dtype),
+        in_specs=[pl.BlockSpec(memory_space=pltpu.VMEM)],
+        out_specs=pl.BlockSpec(memory_space=pltpu.VMEM),
+        scratch_shapes=[
+            pltpu.SemaphoreType.DMA((n,)),
+            pltpu.SemaphoreType.DMA((n,)),
+            pltpu.SemaphoreType.DMA((n,)),
+            pltpu.SemaphoreType.DMA((n,)),
+            pltpu.SemaphoreType.DMA,
+        ],
+        compiler_params=pltpu.CompilerParams(
+            collective_id=1, has_side_effects=True, vmem_limit_bytes=24 * MIB
+        ),
+        name="deliver_embeddings",
+    )(blocks)
+
+
+def value_kernel(partial_ref, embed_ref, gain_ref, out_ref, landed, send_sem, recv_sem):
+    me = lax.axis_index("member")
+    core = lax.axis_index("mp")
+    partner = (me, 1 - core)
+    barrier = pltpu.get_barrier_semaphore()
+    pl.semaphore_signal(barrier, inc=1, device_id=partner, device_id_type=MESH)
+    pl.semaphore_wait(barrier, 1)
+    share_rows = landed.shape[0]
+    parts = 4
+    piece = share_rows // parts
+
+    def copy(i):
+        theirs = pl.multiple_of((1 - core) * share_rows + i * piece, 8)
+        return pltpu.make_async_remote_copy(
+            src_ref=partial_ref.at[pl.ds(theirs, piece)],
+            dst_ref=landed.at[pl.ds(i * piece, piece)],
+            send_sem=send_sem.at[i],
+            recv_sem=recv_sem.at[i],
+            device_id=partner,
+            device_id_type=MESH,
+        )
+
+    for i in range(parts):
+        copy(i).start()
+    for i in range(parts):
+        copy(i).wait_recv()
+        ours = pl.ds(pl.multiple_of(core * share_rows + i * piece, piece), piece)
+        rows = (
+            embed_ref[ours, :].astype(jnp.float32)
+            + partial_ref[ours, :]
+            + landed[i * piece : (i + 1) * piece, :]
+        )
+        scale = lax.rsqrt(jnp.mean(rows * rows, axis=1, keepdims=True) + EPSILON)
+        out_ref[i * piece : (i + 1) * piece, :] = jnp.sum(
+            rows * scale * gain_ref[...], axis=1, keepdims=True
+        )
+    for i in range(parts):
+        copy(i).wait_send()
+
+
+def value_rows_of(partial, embed, gain):
+    rows, width = partial.shape
+    return pl.pallas_call(
+        value_kernel,
+        out_shape=jax.ShapeDtypeStruct((rows // 2, 1), jnp.float32),
+        in_specs=[pl.BlockSpec(memory_space=pltpu.VMEM)] * 3,
+        out_specs=pl.BlockSpec(memory_space=pltpu.VMEM),
+        scratch_shapes=[
+            pltpu.VMEM((rows // 2, width), jnp.float32),
+            pltpu.SemaphoreType.DMA((4,)),
+            pltpu.SemaphoreType.DMA((4,)),
+        ],
+        compiler_params=pltpu.CompilerParams(
+            collective_id=2, has_side_effects=True, vmem_limit_bytes=32 * MIB
+        ),
+        name="value_rows",
+    )(partial, embed, gain[None, :])
+
+
+def on_device_direct(
+    token_ids,
+    fit_ranks,
+    embed_table,
+    norm_gain,
+    qkv_weight,
+    qkv_bias,
+    out_weight,
+    value_weight,
+    qkv_left,
+    qkv_right,
+    out_left,
+    out_right,
+):
+    members, length = token_ids.shape
+    row_count = members * length
+    n = lax.axis_size("member")
+    mp_size = lax.axis_size("mp")
+    heads_here = HQ // mp_size
+    kv_here = HK // mp_size
+    population = members * n
+    features = embed_table.shape[0]
+    half = row_count // mp_size
+    width_in = qkv_weight.shape[1]
+    width_out = out_weight.shape[1]
+    mp_index = lax.axis_index("mp")
+    contract_rows = (((0,), (0,)), ((), ()))
+    weights = lax.all_gather(
+        jnp.concatenate([qkv_weight, out_weight], axis=1), "member", axis=0, tiled=True
+    )
+    id_rows = token_ids.reshape(mp_size, half)
+    rank_row = jnp.zeros((1, half), jnp.int32).at[0, :members].set(fit_ranks)
+    ids = jnp.concatenate([id_rows, rank_row, jnp.zeros((8 - mp_size - 1, half), jnp.int32)])
+
+    def per_owner(factor):
+        return factor.reshape(members, n, features).transpose(1, 0, 2).reshape(n, -1)
+
+    common = jnp.concatenate([qkv_right.reshape(-1), out_left.reshape(-1)])
+    pack = jnp.concatenate(
+        [
+            per_owner(qkv_left),
+            per_owner(out_right),
+            jnp.broadcast_to(common[None, :], (n, common.shape[0])),
+        ],
+        axis=1,
+    )
+    used = pack.shape[1]
+    lines = -(-used // (16 * 128)) * 16
+    pack = jnp.pad(pack, ((0, 0), (0, lines * 128 - used))).reshape(n, lines, 128)
+    all_ids, all_pack = share(ids, pack, n)
+    picked_ids = lax.dynamic_index_in_dim(all_ids, mp_index, 1, keepdims=False).reshape(-1)
+    all_ranks = all_ids[:, mp_size, :members].reshape(-1)
+    embedded = deliver(pick_columns(embed_table, picked_ids, half), n)
+
+    rows = embedded.T
+    states = rows.astype(jnp.float32)
+    inverse_rms = lax.rsqrt(jnp.mean(states * states, axis=1, keepdims=True) + EPSILON)
+    normed = (states * inverse_rms * norm_gain[None, :]).astype(jnp.bfloat16)
+    base_proj = jnp.dot(normed, weights[:, :width_in], preferred_element_type=jnp.float32)
+    coef_in = jnp.einsum(
+        "msd,md->ms",
+        normed.reshape(members, length, -1),
+        qkv_left,
+        preferred_element_type=jnp.float32,
+    )
+    projected = (
+        base_proj.reshape(members, length, -1)
+        + SIGMA * coef_in[:, :, None] * qkv_right.astype(jnp.float32)[:, None, :]
+        + qkv_bias[None, None, :]
+    )
+    query_width = heads_here * HD
+    kv_width = kv_here * HD
+    cosine, sine_table = rope_tables(length, HD)
+    query_heads = rotate(
+        projected[:, :, :query_width].reshape(members, length, heads_here, HD), cosine, sine_table
+    ).astype(jnp.bfloat16)
+    key_heads = rotate(
+        projected[:, :, query_width : query_width + kv_width].reshape(members, length, kv_here, HD),
+        cosine,
+        sine_table,
+    ).astype(jnp.bfloat16)
+    value_heads = (
+        projected[:, :, query_width + kv_width :]
+        .reshape(members, length, kv_here, HD)
+        .astype(jnp.bfloat16)
+    )
+    context = attend(query_heads, key_heads, value_heads, kv_here)
+    coef_out = jnp.einsum("msq,mq->ms", context, out_left, preferred_element_type=jnp.float32)
+    partial_out = lax.dot_general(
+        context.reshape(row_count, query_width),
+        weights[:, width_in:],
+        (((1,), (1,)), ((), ())),
+        preferred_element_type=jnp.float32,
+    )
+    head_term = (
+        partial_out.reshape(members, length, -1)
+        + SIGMA * coef_out[:, :, None] * out_right.astype(jnp.float32)[:, None, :]
+    )
+    value_rows = value_rows_of(head_term.reshape(row_count, -1), rows, value_weight).reshape(
+        members // mp_size, length
+    )
+
+    rank_values = all_ranks.astype(jnp.float32)
+    center = jnp.sum(rank_values) / population
+    spread = jnp.sum(rank_values * rank_values) / population - center * center
+    fitness = (rank_values - center) * lax.rsqrt(spread + EPSILON)
+    flat = all_pack.reshape(n, -1)
+    edge = 0
+    factors = []
+    for width in (features, features, width_in, width_out):
+        piece = flat[:, edge : edge + members * width]
+        factors.append(piece.reshape(population, width).astype(jnp.float32))
+        edge += members * width
+    left_rows, right_rows, right_cols, left_cols = factors
+    grads = [
+        lax.dot_general(
+            mine * fitness[:, None],
+            theirs,
+            contract_rows,
+            precision=lax.Precision.HIGHEST,
+            preferred_element_type=jnp.float32,
+        )
+        / (population * SIGMA)
+        for mine, theirs in ((left_rows, right_cols), (right_rows, left_cols))
+    ]
+    return (value_rows, grads[0], grads[1])
+
+
+def fits_direct(mesh):
+    return mesh.shape["mp"] == 2 and mesh.shape["member"] == 16
+
+
 def solution(mesh):
     placed = (
         P("member", None),
@@ -181,7 +619,7 @@
         P("member", None),
     )
     return jax.shard_map(
-        on_device,
+        on_device_direct if fits_direct(mesh) else on_device,
         mesh=mesh,
         in_specs=placed,
         out_specs=(P(("member", "mp"), None), P("member", "mp"), P("member", "mp")),

time: 449 us -> 241 us (0.54)
  blocking collectives: 197 us -> 0 us
  local copies, waits for them, and re-layouts: 119 us -> 16.4 us
  Pallas kernels: 0 us -> 96.9 us
  starting transfers between devices: 11.4 us -> 0.04 us
  waiting for transfers between devices: 66.2 us -> 77 us
    all_gather x3 -> x0, blocking collectives: 118 us -> none  [the longest x1 43.4 us: on_device(): all_ids = lax.all_gather(token_ids, 'member', axis=0, tiled=True)]
    pallas_call x0 -> x4, Pallas kernels: none -> 96.9 us  [the longest x1 36.3 us: deliver(): pl.pallas_call(functools.partial(deliver_kernel, n), out_shape=jax.ShapeD...]
    all_gather x2 -> x1, waiting for transfers between devices: 5.99 us -> 77 us  [on_device_direct(): lax.all_gather(jnp.concatenate([qkv_weight, out_weight], axis=1), 'member...]
    all_to_all x3 -> x0, waiting for transfers between devices: 58.8 us -> none  [the longest x1 51.5 us: on_device(): lax.all_to_all(picked, 'member', split_axis=1, concat_axis=0, tiled=True)]
    gather x2 -> x0, local copies, waits for them, and re-layouts: 46.5 us -> none  [on_device(): picked = jnp.take(embed_table, all_ids.reshape(-1), axis=1)]
    psum x1 -> x0, blocking collectives: 42.7 us -> none  [on_device(): lax.psum((jnp.sum(rank_values), jnp.sum(rank_values * rank_values)), 'mem...]
    unnamed x27 -> x23, local copies, waits for them, and re-layouts: 46.3 us -> 4.56 us
    unnamed x1 -> x0, blocking collectives: 36.5 us -> none
  transfers between devices with their start and end apart: 6 -> 1, of which waited for: 3 -> 1; matrix products, arithmetic and copies ran while one was open for 31% -> 10% of each run, Pallas kernels for 0% -> 39%
where the time goes in v1:
time: 241 us; the launch traced here: 240 us
  Pallas kernels  96.9 us (40%)
  waiting for transfers between devices  77 us (32%)
  matrix products  17.9 us (7%)
  between operations  17.1 us (7%)
  local copies, waits for them, and re-layouts  16.4 us (7%)
  other arithmetic  14.3 us (6%)
    all_gather x1, waiting for transfers between devices, on_device_direct(): lax.all_gather(jnp.concatenate([qkv_weight, out_weight], axis=1), 'member...  77 us
    pallas_call x1, Pallas kernels, deliver(): pl.pallas_call(functools.partial(deliver_kernel, n), out_shape=jax.ShapeD...  36.3 us
    pallas_call x1, Pallas kernels, pick_columns(): pl.pallas_call(pick_kernel, out_shape=jax.ShapeDtypeStruct((picks // bloc...  33.9 us
    pallas_call x1, Pallas kernels, share(): pl.pallas_call(functools.partial(share_kernel, n), out_shape=(jax.ShapeDt...  22.6 us
    dot_general x1, matrix products, on_device_direct(): jnp.dot(normed, weights[:, :width_in], preferred_element_type=jnp.float32)  6.46 us
    dot_general x1, matrix products, on_device_direct(): lax.dot_general(context.reshape(row_count, query_width), weights[:, width...  4.94 us
  transfers between devices with their start and end apart: 1, of which 1 were waited for; matrix products, arithmetic and copies ran while one was open for 10% of the time, Pallas kernels for 39%

profile of v1, /device:TPU:0, one launch (start us, length us, event | category | flops | bytes accessed | tf_op | source)
XLA Modules:
  0.0 239.6 jit_solution(2886972788276798393)
XLA Ops:
  7.2 2.2 pad_maximum_fusion
  10.9 0.9 reshape.231
  17.3 22.6 %share_small.1 = (s32[16,8,128]{2,1,0:T(8,128)}, bf16[16,80,128]{2,1,0:T(8,128)(2,1)}) custom-call(s32[8,128]{1,0:T(8,128)} %fusion.30.ids_ref, bf16[16,80,128]{2,1,0:T(8,128)(2,1)} %bitcast.78), custom_call_target="tpu_custom_call" | custom-call | tf_op jit(solution)/shard_map/share_small/pallas_call | solution.py:233
  39.9 1.1 copy.67
  41.0 0.9 constant_dynamic-slice_fusion
  42.0 1.8 convert_reduce_fusion
  43.8 1.7 select_reduce_fusion
  45.6 33.9 %pick_columns.1.blocks_ref = bf16[16,224,128]{2,1,0:T(8,128)(2,1)S(1)} custom-call(s32[34]{0:T(128)S(1)} %convert_reduce_fusion.1.count_ref, s32[1,2048]{1,0:T(1,128)S(1)} %bitcast.76, s32[1,2048]{1,0:T(1,128)S(1)} %bitcast.75, bf16[224,76032]{1,0:T(8,128)(2,1)} %table_ref.1), custom_call_target="tpu_custom_call" | custom-call | flops 8719958016 | bytes 34062336 | tf_op jit(solution)/shard_map/pick_columns/pallas_call | solution.py:299
  79.5 36.3 %deliver_embeddings.1 = bf16[3584,256]{1,0:T(8,128)(2,1)S(1)} custom-call(bf16[16,224,128]{2,1,0:T(8,128)(2,1)S(1)} %pick_columns.1.blocks_ref), custom_call_target="tpu_custom_call" | custom-call | tf_op jit(solution)/shard_map/deliver_embeddings/pallas_call | solution.py:396
  115.8 1.2 copy-done
  117.0 2.9 %copy.42 = bf16[3584,256]{0,1:T(8,128)(2,1)S(1)} copy(bf16[3584,256]{1,0:T(8,128)(2,1)} %copy-done) | data formatting | bytes 3670016 | tf_op jit(solution)/shard_map/deliver_embeddings/pallas_call | solution.py:396
  120.0 1.5 convert_reduce_fusion.2
  124.1 0.9 subtract_multiply_fusion
  126.8 1.2 copy-done.2
  128.7 1.4 convolution_multiply_fusion.2
  130.1 1.6 convolution_multiply_fusion
  131.7 77.0 %all-gather.2.cloned.1.call-done = bf16[3584,2048]{1,0:T(8,128)(2,1)} async-done(((bf16[224,2048]{1,0:T(8,128)(2,1)}), bf16[3584,2048]{1,0:T(8,128)(2,1)}) %all-gather.2.cloned.1.call-update) | async-done | bytes 14680080 | tf_op jit(solution)/shard_map/all_gather | solution.py:501
  208.6 6.5 %fusion = f32[256,1152]{1,0:T(8,128)S(1)} fusion(bf16[256,3584]{1,0:T(8,128)(2,1)} %copy-done.2, bf16[3584,2048]{1,0:T(8,128)(2,1)} %all-gather.2.cloned.1.call-done), kind=kOutput, calls=%fused_computation.3 | convolution fusion | flops 2113929216 | bytes 11272192 | tf_op jit(solution)/shard_map/dot_general | solution.py:532
  215.3 1.1 slice.78
  216.7 1.3 reshape.239
  218.8 1.5 fusion.33
  220.5 1.2 fusion.9
  222.9 4.9 %fusion.3 = f32[4,64,3584]{2,1,0:T(8,128)S(1)} fusion(bf16[4,64,896]{2,1,0:T(8,128)(2,1)S(1)} %dot_general.30, bf16[3584,2048]{1,0:T(8,128)(2,1)} %all-gather.2.cloned.1.call-done, f32[4,3584]{1,0:T(4,128)S(1)} %convert_element_type.74, f32[4,64]{1,0:T(4,128)S(1)} %broadcast_multiply_fusion), kind=kOutput, calls=%fused_computation.7 | convolution fusion | flops 1646002176 | bytes 10609664 | tf_op jit(solution)/shard_map/dot_general | solution.py:562
  227.8 4.2 %value_rows.1 = f32[128,1]{1,0:T(8,128)S(1)} custom-call(f32[256,3584]{1,0:T(8,128)S(1)} %bitcast.74, bf16[256,3584]{1,0:T(8,128)(2,1)S(1)} %bitcast.73, f32[1,3584]{1,0:T(1,128)S(1)} %broadcast_in_dim.38.gain_ref), custom_call_target="tpu_custom_call" | custom-call | tf_op jit(solution)/shard_map/value_rows/pallas_call | solution.py:457
  (73 shorter events, 12.9 us)
Async XLA Ops:
  7.2 8.1 %copy-start.8 = (s32[4,64]{1,0:T(4,128)S(1)}, s32[4,64]{1,0:T(4,128)}, u32[]{:S(2)}) copy-start(s32[4,64]{1,0:T(4,128)} %param.14) | copy-start | bytes 3076
  7.2 8.8 %copy-start.9 = (s32[4]{0:T(128)S(1)}, s32[4]{0:T(128)}, u32[]{:S(2)}) copy-start(s32[4]{0:T(128)} %param.15) | copy-start | bytes 52
  7.2 201.4 %all-gather.2.cloned.1.call-start = ((), (), s32[]{:S(2)}) async-start(), calls=%async_computation | async-start | bytes 15597568 | tf_op jit(solution)/shard_map/all_gather | solution.py:501
  79.4 40.5 %copy-start.5 = (f32[3584]{0:T(1024)S(1)}, f32[3584]{0:T(1024)}, u32[]{:S(2)}) copy-start(f32[3584]{0:T(1024)} %param.21) | copy-start | bytes 43012
  115.7 1.2 copy-start
  117.0 9.3 %copy-start.4 = (f32[3584]{0:T(1024)S(1)}, f32[3584]{0:T(1024)}, u32[]{:S(2)}) copy-start(f32[3584]{0:T(1024)} %param.17) | copy-start | bytes 43012
  120.0 8.1 %copy-start.3 = (bf16[4,3584]{1,0:T(4,128)(2,1)S(1)}, bf16[4,3584]{1,0:T(4,128)(2,1)}, u32[]{:S(2)}) copy-start(bf16[4,3584]{1,0:T(4,128)(2,1)} %param.22) | copy-start | bytes 86020
  126.8 1.2 copy-start.2
  131.7 83.4 %copy-start.6 = (f32[1152]{0:T(1024)S(1)}, f32[1152]{0:T(1024)}, u32[]{:S(2)}) copy-start(f32[1152]{0:T(1024)} %param.19) | copy-start | bytes 13828
  215.3 1.3 copy-start.1
  220.3 2.3 copy-start.7
Sparse Core Ops, SparseCore 0:
  10.8 197.8 all-gather.1

commit v2 on v1

--- a/solution.py
+++ b/solution.py
@@ -171,6 +171,8 @@
 MESH = pl.DeviceIdType.MESH
 VOCAB_BLOCK = 2304
 GROUP = 256
+PLANE = 4
+RELAYED = 5 * HD
 MIB = 1024 * 1024
 
 
@@ -322,7 +324,24 @@
     )(counts, ordered[None, :], ranks[None, :], table)
 
 
-def deliver_kernel(n, blocks_ref, out_ref, send_sem, recv_sem, pass_send, pass_recv, own_sem):
+def deliver_kernel(
+    n,
+    blocks_ref,
+    weight_ref,
+    out_ref,
+    all_ref,
+    send_sem,
+    recv_sem,
+    pass_send,
+    pass_recv,
+    own_sem,
+    line_send,
+    line_recv,
+    side_send,
+    side_recv,
+    far_send,
+    far_recv,
+):
     me = lax.axis_index("member")
     core = lax.axis_index("mp")
     features, block = blocks_ref.shape[1:]
@@ -363,14 +382,68 @@
             device_id_type=MESH,
         )
 
+    layer = me // PLANE
+    spot = lax.rem(me, PLANE)
+    depth = n // PLANE
+    half_rows = weight_ref.shape[0] // 2
+    flips = (lax.rem(spot, 2), spot // 2)
+    beside = (spot + 1 - 2 * flips[0], spot + 2 - 4 * flips[1])
+
+    def owner(k, where):
+        return lax.rem(layer + depth - k, depth) * PLANE + where
+
+    def along(k):
+        other = lax.rem(layer + k, depth) * PLANE + spot
+        return pltpu.make_async_remote_copy(
+            src_ref=weight_ref,
+            dst_ref=all_ref.at[me],
+            send_sem=line_send.at[k],
+            recv_sem=line_recv.at[k],
+            device_id=(other, core),
+            device_id_type=MESH,
+        )
+
+    def aside(side, k):
+        source = owner(k, spot)
+        return pltpu.make_async_remote_copy(
+            src_ref=weight_ref if k == 0 else all_ref.at[source],
+            dst_ref=all_ref.at[source],
+            send_sem=side_send.at[side, k],
+            recv_sem=side_recv.at[side, k],
+            device_id=(layer * PLANE + beside[side], core),
+            device_id_type=MESH,
+        )
+
+    def onward(side, k):
+        piece = all_ref.at[owner(k, beside[side]), pl.ds(side * half_rows, half_rows)]
+        return pltpu.make_async_remote_copy(
+            src_ref=piece,
+            dst_ref=piece,
+            send_sem=far_send.at[side, k],
+            recv_sem=far_recv.at[side, k],
+            device_id=(layer * PLANE + beside[1 - side], core),
+            device_id_type=MESH,
+        )
+
+    for k in range(1, depth):
+        along(k).start()
+
     def launch(k, carry):
         across(k).start()
         return carry
 
     lax.fori_loop(1, n, launch, 0)
     over(0, blocks_ref.at[me], me).start()
-    own = pltpu.make_async_copy(blocks_ref.at[me], place(me), own_sem)
+    own = pltpu.make_async_copy(blocks_ref.at[me], place(me), own_sem.at[0])
     own.start()
+    own_weight = pltpu.make_async_copy(weight_ref, all_ref.at[me], own_sem.at[1])
+    own_weight.start()
+    for side in range(2):
+        aside(side, 0).start()
+    for k in range(1, depth):
+        along(k).wait_recv()
+        for side in range(2):
+            aside(side, k).start()
 
     def forward(k, carry):
         across(k).wait_recv()
@@ -379,7 +452,12 @@
         return carry
 
     lax.fori_loop(1, n, forward, 0)
+    for k in range(depth):
+        for side in range(2):
+            aside(side, k).wait_recv()
+            onward(side, k).start()
     own.wait()
+    own_weight.wait()
     over(0, blocks_ref.at[me], me).wait()
 
     def finish(k, carry):
@@ -389,27 +467,42 @@
         return carry
 
     lax.fori_loop(1, n, finish, 0)
-
-
-def deliver(blocks, n):
+    for k in range(1, depth):
+        along(k).wait_send()
+    for k in range(depth):
+        for side in range(2):
+            aside(side, k).wait_send()
+            onward(side, k).wait()
+
+
+def deliver(blocks, weight, n):
     _, features, block = blocks.shape
     return pl.pallas_call(
         functools.partial(deliver_kernel, n),
-        out_shape=jax.ShapeDtypeStruct((n * features, 2 * block), blocks.dtype),
-        in_specs=[pl.BlockSpec(memory_space=pltpu.VMEM)],
-        out_specs=pl.BlockSpec(memory_space=pltpu.VMEM),
+        out_shape=(
+            jax.ShapeDtypeStruct((n * features, 2 * block), blocks.dtype),
+            jax.ShapeDtypeStruct((n,) + weight.shape, weight.dtype),
+        ),
+        in_specs=[pl.BlockSpec(memory_space=pltpu.VMEM), pl.BlockSpec(memory_space=pl.ANY)],
+        out_specs=[pl.BlockSpec(memory_space=pltpu.VMEM), pl.BlockSpec(memory_space=pl.ANY)],
         scratch_shapes=[
             pltpu.SemaphoreType.DMA((n,)),
             pltpu.SemaphoreType.DMA((n,)),
             pltpu.SemaphoreType.DMA((n,)),
             pltpu.SemaphoreType.DMA((n,)),
-            pltpu.SemaphoreType.DMA,
+            pltpu.SemaphoreType.DMA((2,)),
+            pltpu.SemaphoreType.DMA((n // PLANE,)),
+            pltpu.SemaphoreType.DMA((n // PLANE,)),
+            pltpu.SemaphoreType.DMA((2, n // PLANE)),
+            pltpu.SemaphoreType.DMA((2, n // PLANE)),
+            pltpu.SemaphoreType.DMA((2, n // PLANE)),
+            pltpu.SemaphoreType.DMA((2, n // PLANE)),
         ],
         compiler_params=pltpu.CompilerParams(
             collective_id=1, has_side_effects=True, vmem_limit_bytes=24 * MIB
         ),
         name="deliver_embeddings",
-    )(blocks)
+    )(blocks, weight)
 
 
 def value_kernel(partial_ref, embed_ref, gain_ref, out_ref, landed, send_sem, recv_sem):
@@ -498,8 +591,9 @@
     width_out = out_weight.shape[1]
     mp_index = lax.axis_index("mp")
     contract_rows = (((0,), (0,)), ((), ()))
+    kept = width_out - RELAYED
     weights = lax.all_gather(
-        jnp.concatenate([qkv_weight, out_weight], axis=1), "member", axis=0, tiled=True
+        jnp.concatenate([qkv_weight, out_weight[:, :kept]], axis=1), "member", axis=0, tiled=True
     )
     id_rows = token_ids.reshape(mp_size, half)
     rank_row = jnp.zeros((1, half), jnp.int32).at[0, :members].set(fit_ranks)
@@ -523,7 +617,9 @@
     all_ids, all_pack = share(ids, pack, n)
     picked_ids = lax.dynamic_index_in_dim(all_ids, mp_index, 1, keepdims=False).reshape(-1)
     all_ranks = all_ids[:, mp_size, :members].reshape(-1)
-    embedded = deliver(pick_columns(embed_table, picked_ids, half), n)
+    embedded, relayed = deliver(
+        pick_columns(embed_table, picked_ids, half), out_weight[:, kept:], n
+    )
 
     rows = embedded.T
     states = rows.astype(jnp.float32)
@@ -559,10 +655,17 @@
     )
     context = attend(query_heads, key_heads, value_heads, kv_here)
     coef_out = jnp.einsum("msq,mq->ms", context, out_left, preferred_element_type=jnp.float32)
+    flat_context = context.reshape(row_count, query_width)
+    contract_cols = (((1,), (1,)), ((), ()))
     partial_out = lax.dot_general(
-        context.reshape(row_count, query_width),
+        flat_context[:, :kept],
         weights[:, width_in:],
-        (((1,), (1,)), ((), ())),
+        contract_cols,
+        preferred_element_type=jnp.float32,
+    ) + lax.dot_general(
+        flat_context[:, kept:],
+        relayed.reshape(n * features, -1),
+        contract_cols,
         preferred_element_type=jnp.float32,
     )
     head_term = (

time: 241 us -> 250 us (1.037)
  the two profiles are of different devices: /device:TPU:0 before, /device:TPU:27 now
where the time goes in v2:
time: 250 us; the launch traced here: 249 us
  Pallas kernels  178 us (71%)
  local copies, waits for them, and re-layouts  20.6 us (8%)
  matrix products  19.1 us (8%)
  between operations  17.1 us (7%)
  other arithmetic  14.5 us (6%)
    pallas_call x1, Pallas kernels, deliver(): pl.pallas_call(functools.partial(deliver_kernel, n), out_shape=(jax.Shape...  117 us
    pallas_call x1, Pallas kernels, pick_columns(): pl.pallas_call(pick_kernel, out_shape=jax.ShapeDtypeStruct((picks // bloc...  34.2 us
    pallas_call x1, Pallas kernels, share(): pl.pallas_call(functools.partial(share_kernel, n), out_shape=(jax.ShapeDt...  21.8 us
    unnamed x26, local copies, waits for them, and re-layouts  6.82 us
    dot_general x1, matrix products, on_device_direct(): jnp.dot(normed, weights[:, :width_in], preferred_element_type=jnp.float32)  6.46 us
  transfers between devices with their start and end apart: 1, of which 0 were waited for; matrix products, arithmetic and copies ran while one was open for 10% of the time, Pallas kernels for 69%

profile of v2, /device:TPU:27, one launch (start us, length us, event | category | flops | bytes accessed | tf_op | source)
XLA Modules:
  0.0 248.8 jit_solution(6205517328533298424)
XLA Ops:
  7.2 0.9 slice.72
  8.1 1.9 pad_maximum_fusion
  10.1 1.0 slice.71.weight_ref
  18.9 21.8 %share_small.1 = (s32[16,8,128]{2,1,0:T(8,128)}, bf16[16,80,128]{2,1,0:T(8,128)(2,1)}) custom-call(s32[8,128]{1,0:T(8,128)} %fusion.33.ids_ref, bf16[16,80,128]{2,1,0:T(8,128)(2,1)} %bitcast.84), custom_call_target="tpu_custom_call" | custom-call | tf_op jit(solution)/shard_map/share_small/pallas_call | solution.py:235
  40.7 1.1 copy.73
  42.9 1.8 convert_reduce_fusion
  44.7 1.7 select_reduce_fusion
  46.4 34.2 %pick_columns.1.blocks_ref = bf16[16,224,128]{2,1,0:T(8,128)(2,1)S(1)} custom-call(s32[34]{0:T(128)S(1)} %convert_reduce_fusion.1.count_ref, s32[1,2048]{1,0:T(1,128)S(1)} %bitcast.79, s32[1,2048]{1,0:T(1,128)S(1)} %bitcast.78, bf16[224,76032]{1,0:T(8,128)(2,1)} %table_ref.1), custom_call_target="tpu_custom_call" | custom-call | flops 8719958016 | bytes 34062336 | tf_op jit(solution)/shard_map/pick_columns/pallas_call | solution.py:301
  80.6 116.9 %deliver_embeddings.1 = (bf16[3584,256]{1,0:T(8,128)(2,1)S(1)}, bf16[16,224,640]{2,1,0:T(8,128)(2,1)S(1)}) custom-call(bf16[16,224,128]{2,1,0:T(8,128)(2,1)S(1)} %pick_columns.1.blocks_ref, bf16[224,640]{1,0:T(8,128)(2,1)S(1)} %slice.71.weight_ref), custom_call_target="tpu_custom_call" | custom-call | tf_op jit(solution)/shard_map/deliver_embeddings/pallas_call | solution.py:480
  197.5 2.2 copy-done
  199.7 1.2 copy-done.1
  201.0 2.9 %copy.44 = bf16[3584,256]{0,1:T(8,128)(2,1)S(1)} copy(bf16[3584,256]{1,0:T(8,128)(2,1)} %copy-done.1) | data formatting | bytes 3670016 | tf_op jit(solution)/shard_map/deliver_embeddings/pallas_call | solution.py:480
  204.0 1.5 convert_reduce_fusion.2
  210.8 1.2 copy-done.3
  212.6 1.4 convolution_multiply_fusion.2
  214.0 1.6 convolution_multiply_fusion
  215.6 6.5 %fusion = f32[256,1152]{1,0:T(8,128)S(1)} fusion(bf16[256,3584]{1,0:T(8,128)(2,1)} %copy-done.3, bf16[3584,1408]{1,0:T(8,128)(2,1)} %all-gather.2.cloned.1.call-done), kind=kOutput, calls=%fused_computation.3 | convolution fusion | flops 2113929216 | bytes 11272192 | tf_op jit(solution)/shard_map/dot_general | solution.py:628
  222.3 1.1 slice.94
  223.6 1.3 reshape.243
  225.8 1.5 fusion.36
  227.5 1.2 fusion.9
  230.0 3.9 %fusion.15 = f32[256,3584]{1,0:T(8,128)S(1)} fusion(bf16[3584,640]{1,0:T(8,128)(2,1)} %bitcast.77, bf16[256,896]{1,0:T(8,128)(2,1)S(1)} %bitcast.81), kind=kOutput, calls=%fused_computation.34 | convolution fusion | flops 1174405120 | bytes 8585216 | tf_op jit(solution)/shard_map/dot_general | solution.py:665
  234.4 2.2 fusion.2.partial_ref
  236.6 4.7 %value_rows.1 = f32[128,1]{1,0:T(8,128)S(1)} custom-call(f32[256,3584]{1,0:T(8,128)S(1)} %fusion.2.partial_ref, bf16[256,3584]{1,0:T(8,128)(2,1)S(1)} %bitcast.76, f32[1,3584]{1,0:T(1,128)S(1)} %broadcast_in_dim.38.gain_ref), custom_call_target="tpu_custom_call" | custom-call | tf_op jit(solution)/shard_map/value_rows/pallas_call | solution.py:550
  (81 shorter events, 16.0 us)
Async XLA Ops:
  7.2 9.7 %copy-start.9 = (s32[4,64]{1,0:T(4,128)S(1)}, s32[4,64]{1,0:T(4,128)}, u32[]{:S(2)}) copy-start(s32[4,64]{1,0:T(4,128)} %param.14) | copy-start | bytes 3076
  7.2 10.4 %copy-start.10 = (s32[4]{0:T(128)S(1)}, s32[4]{0:T(128)}, u32[]{:S(2)}) copy-start(s32[4]{0:T(128)} %param.15) | copy-start | bytes 52
  7.2 208.4 %all-gather.2.cloned.1.call-start = ((), (), s32[]{:S(2)}) async-start(), calls=%async_computation | async-start | bytes 10723328 | tf_op jit(solution)/shard_map/all_gather | solution.py:595
  80.6 123.3 %copy-start.6 = (f32[3584]{0:T(1024)S(1)}, f32[3584]{0:T(1024)}, u32[]{:S(2)}) copy-start(f32[3584]{0:T(1024)} %param.21) | copy-start | bytes 43012
  197.5 2.2 copy-start
  199.7 1.2 copy-start.1
  201.0 9.3 %copy-start.5 = (f32[3584]{0:T(1024)S(1)}, f32[3584]{0:T(1024)}, u32[]{:S(2)}) copy-start(f32[3584]{0:T(1024)} %param.17) | copy-start | bytes 43012
  203.9 8.1 %copy-start.4 = (bf16[4,3584]{1,0:T(4,128)(2,1)S(1)}, bf16[4,3584]{1,0:T(4,128)(2,1)}, u32[]{:S(2)}) copy-start(bf16[4,3584]{1,0:T(4,128)(2,1)} %param.22) | copy-start | bytes 86020
  210.7 1.2 copy-start.3
  215.6 6.5 %copy-start.7 = (f32[1152]{0:T(1024)S(1)}, f32[1152]{0:T(1024)}, u32[]{:S(2)}) copy-start(f32[1152]{0:T(1024)} %param.19) | copy-start | bytes 13828
  222.3 1.3 copy-start.2
  227.3 2.4 copy-start.8
Sparse Core Ops, SparseCore 0:
  10.7 176.6 all-gather.1

commit v3 on v2

--- a/solution.py
+++ b/solution.py
@@ -172,7 +172,7 @@
 VOCAB_BLOCK = 2304
 GROUP = 256
 PLANE = 4
-RELAYED = 5 * HD
+RELAYED = 3 * HD
 MIB = 1024 * 1024
 
 

time: 250 us -> 227 us (0.908)
  the two profiles are of different devices: /device:TPU:27 before, /device:TPU:0 now
where the time goes in v3:
time: 227 us; the launch traced here: 226 us
  Pallas kernels  136 us (60%)
  waiting for transfers between devices  20.4 us (9%)
  local copies, waits for them, and re-layouts  20.1 us (9%)
  matrix products  17.5 us (8%)
  between operations  17.1 us (8%)
  other arithmetic  14.6 us (6%)
    pallas_call x1, Pallas kernels, deliver(): pl.pallas_call(functools.partial(deliver_kernel, n), out_shape=(jax.Shape...  75.9 us
    pallas_call x1, Pallas kernels, pick_columns(): pl.pallas_call(pick_kernel, out_shape=jax.ShapeDtypeStruct((picks // bloc...  34 us
    pallas_call x1, Pallas kernels, share(): pl.pallas_call(functools.partial(share_kernel, n), out_shape=(jax.ShapeDt...  22.1 us
    all_gather x1, waiting for transfers between devices, on_device_direct(): lax.all_gather(jnp.concatenate([qkv_weight, out_weight[:, :kept]], axis=1...  20.4 us
    dot_general x1, matrix products, on_device_direct(): jnp.dot(normed, weights[:, :width_in], preferred_element_type=jnp.float32)  6.46 us
    unnamed x28, local copies, waits for them, and re-layouts  6.24 us
  transfers between devices with their start and end apart: 1, of which 1 were waited for; matrix products, arithmetic and copies ran while one was open for 11% of the time, Pallas kernels for 58%

profile of v3, /device:TPU:0, one launch (start us, length us, event | category | flops | bytes accessed | tf_op | source)
XLA Modules:
  0.0 225.8 jit_solution(8757129011706620857)
XLA Ops:
  7.2 1.0 slice.72
  8.2 2.0 pad_maximum_fusion
  19.0 22.1 %share_small.1 = (s32[16,8,128]{2,1,0:T(8,128)}, bf16[16,80,128]{2,1,0:T(8,128)(2,1)}) custom-call(s32[8,128]{1,0:T(8,128)} %fusion.33.ids_ref, bf16[16,80,128]{2,1,0:T(8,128)(2,1)} %bitcast.84), custom_call_target="tpu_custom_call" | custom-call | tf_op jit(solution)/shard_map/share_small/pallas_call | solution.py:235
  41.1 1.1 copy.73
  43.3 1.8 convert_reduce_fusion
  45.1 1.7 select_reduce_fusion
  46.9 34.0 %pick_columns.1.blocks_ref = bf16[16,224,128]{2,1,0:T(8,128)(2,1)S(1)} custom-call(s32[34]{0:T(128)S(1)} %convert_reduce_fusion.1.count_ref, s32[1,2048]{1,0:T(1,128)S(1)} %bitcast.79, s32[1,2048]{1,0:T(1,128)S(1)} %bitcast.78, bf16[224,76032]{1,0:T(8,128)(2,1)} %table_ref.1), custom_call_target="tpu_custom_call" | custom-call | flops 8719958016 | bytes 34062336 | tf_op jit(solution)/shard_map/pick_columns/pallas_call | solution.py:301
  80.9 75.9 %deliver_embeddings.1 = (bf16[3584,256]{1,0:T(8,128)(2,1)S(1)}, bf16[16,224,384]{2,1,0:T(8,128)(2,1)S(1)}) custom-call(bf16[16,224,128]{2,1,0:T(8,128)(2,1)S(1)} %pick_columns.1.blocks_ref, bf16[224,384]{1,0:T(8,128)(2,1)S(1)} %slice.71.weight_ref), custom_call_target="tpu_custom_call" | custom-call | tf_op jit(solution)/shard_map/deliver_embeddings/pallas_call | solution.py:480
  156.8 1.6 copy-done
  158.4 1.2 copy-done.2
  159.6 2.9 %copy.44 = bf16[3584,256]{0,1:T(8,128)(2,1)S(1)} copy(bf16[3584,256]{1,0:T(8,128)(2,1)} %copy-done.2) | data formatting | bytes 3670016 | tf_op jit(solution)/shard_map/deliver_embeddings/pallas_call | solution.py:480
  162.6 1.5 convert_reduce_fusion.2
  169.4 1.2 copy-done.4
  171.2 1.4 convolution_multiply_fusion.2
  172.6 1.6 convolution_multiply_fusion
  174.2 20.4 %all-gather.2.cloned.1.call-done = bf16[3584,1664]{1,0:T(8,128)(2,1)} async-done(((bf16[224,1664]{1,0:T(8,128)(2,1)}), bf16[3584,1664]{1,0:T(8,128)(2,1)}) %all-gather.2.cloned.1.call-update) | async-done | bytes 11927568 | tf_op jit(solution)/shard_map/all_gather | solution.py:595
  194.6 6.5 %fusion = f32[256,1152]{1,0:T(8,128)S(1)} fusion(bf16[256,3584]{1,0:T(8,128)(2,1)} %copy-done.4, bf16[3584,1664]{1,0:T(8,128)(2,1)} %all-gather.2.cloned.1.call-done), kind=kOutput, calls=%fused_computation.3 | convolution fusion | flops 2113929216 | bytes 11272192 | tf_op jit(solution)/shard_map/dot_general | solution.py:628
  201.3 1.1 slice.94
  202.6 1.3 reshape.243
  204.8 1.5 fusion.36
  206.5 1.2 fusion.10
  209.4 3.3 %fusion.6 = f32[256,3584]{1,0:T(8,128)S(1)} fusion(bf16[3584,1664]{1,0:T(8,128)(2,1)} %all-gather.2.cloned.1.call-done, bf16[256,896]{1,0:T(8,128)(2,1)S(1)} %bitcast.82), kind=kOutput, calls=%fused_computation.12 | convolution fusion | flops 939524096 | bytes 7602176 | tf_op jit(solution)/shard_map/dot_general | solution.py:660
  212.8 1.2 fusion.2.partial_ref
  214.0 4.2 %value_rows.1 = f32[128,1]{1,0:T(8,128)S(1)} custom-call(f32[256,3584]{1,0:T(8,128)S(1)} %fusion.2.partial_ref, bf16[256,3584]{1,0:T(8,128)(2,1)S(1)} %bitcast.76, f32[1,3584]{1,0:T(1,128)S(1)} %broadcast_in_dim.38.gain_ref), custom_call_target="tpu_custom_call" | custom-call | tf_op jit(solution)/shard_map/value_rows/pallas_call | solution.py:550
  (83 shorter events, 17.0 us)
Async XLA Ops:
  7.2 9.8 %copy-start.10 = (s32[4,64]{1,0:T(4,128)S(1)}, s32[4,64]{1,0:T(4,128)}, u32[]{:S(2)}) copy-start(s32[4,64]{1,0:T(4,128)} %param.14) | copy-start | bytes 3076
  7.2 10.5 %copy-start.11 = (s32[4]{0:T(128)S(1)}, s32[4]{0:T(128)}, u32[]{:S(2)}) copy-start(s32[4]{0:T(128)} %param.15) | copy-start | bytes 52
  7.2 187.4 %all-gather.2.cloned.1.call-start = ((), (), s32[]{:S(2)}) async-start(), calls=%async_computation | async-start | bytes 12673024 | tf_op jit(solution)/shard_map/all_gather | solution.py:595
  80.8 81.7 %copy-start.7 = (f32[3584]{0:T(1024)S(1)}, f32[3584]{0:T(1024)}, u32[]{:S(2)}) copy-start(f32[3584]{0:T(1024)} %param.21) | copy-start | bytes 43012
  156.7 1.6 copy-start
  158.4 1.2 copy-start.2
  159.6 9.3 %copy-start.6 = (f32[3584]{0:T(1024)S(1)}, f32[3584]{0:T(1024)}, u32[]{:S(2)}) copy-start(f32[3584]{0:T(1024)} %param.17) | copy-start | bytes 43012
  162.6 8.1 %copy-start.5 = (bf16[4,3584]{1,0:T(4,128)(2,1)S(1)}, bf16[4,3584]{1,0:T(4,128)(2,1)}, u32[]{:S(2)}) copy-start(bf16[4,3584]{1,0:T(4,128)(2,1)} %param.22) | copy-start | bytes 86020
  169.4 1.2 copy-start.4
  174.2 26.8 %copy-start.8 = (f32[1152]{0:T(1024)S(1)}, f32[1152]{0:T(1024)}, u32[]{:S(2)}) copy-start(f32[1152]{0:T(1024)} %param.19) | copy-start | bytes 13828
  201.3 1.3 copy-start.3
  206.3 2.4 %copy-start.9 = (bf16[4,896]{1,0:T(4,128)(2,1)S(1)}, bf16[4,896]{1,0:T(4,128)(2,1)}, u32[]{:S(2)}) copy-start(bf16[4,896]{1,0:T(4,128)(2,1)} %param.24) | copy-start | bytes 21508
  209.4 3.4 %copy-start.1 = (bf16[16,224,384]{2,1,0:T(8,128)(2,1)S(1)}, bf16[16,224,384]{2,1,0:T(8,128)(2,1)}, u32[]{:S(2)}) copy-start(bf16[16,224,384]{2,1,0:T(8,128)(2,1)} %copy-done) | copy-start | bytes 8257540
Sparse Core Ops, SparseCore 0:
  10.8 183.7 all-gather.1
